TPU v7x, 32 devices: a whole 2x2x4 slice. The times are simulated.
32 devices in a mesh: tm: 4 (over z), space: 8 (over y, x, core).
Axes of the slice: x: 2, y: 2, z: 4, core: 2. Of those that a mesh axis runs over, the one named last changes fastest.
Arguments:
- snaps: bfloat16 [4096, 3, 16384], P('tm', None, 'space')
- phase_bin: int32 [4096], P('tm'), may hold values from 0 to 15, as said below
- owner_order: int32 [16], replicated, may hold values from 0 to 15, each once
- modes: bfloat16 [16, 128, 3, 16384], P(None, None, None, 'space'), may hold values from -0.02734375 to 0.02734375
Outputs:
- phase_mean: bfloat16 [16, 3, 16384], P('tm', None, 'space')
- coefficients: float32 [4096, 128], P('tm')
Inputs may be any that keep to these rules, and one draw needn't show every extreme that they name: `phase_bin`: every bin is named by at least one snapshot; in each aligned block of 1024 snapshots no bin is named more than 128 times.
All inputs are finite; a program needn't handle non-finite values.
Results may differ from a plain program's by a relative error of at most 0.0068.
Values may be sent and summed in bfloat16 or wider, within the bound.
A program may use at most 192 MiB of HBM per device.

v0:
```python
import jax
import jax.numpy as jnp
from jax import lax
from jax.sharding import PartitionSpec as P


def on_device(snaps, phase_bin, owner_order, modes):
    snap_rows = snaps.shape[0]
    cell_count = snaps.shape[2]
    bin_total = modes.shape[0]
    mode_count = modes.shape[1]
    width = 3 * cell_count
    capacity = 2 * snap_rows // bin_total
    flattened = snaps.reshape(snap_rows, width)
    bin_ids = lax.broadcasted_iota(jnp.int32, (bin_total, 1), 0)
    matches = phase_bin[None, :] == bin_ids
    onehot = matches.astype(jnp.bfloat16)
    reorder = (owner_order[:, None] == bin_ids[:, 0][None, :]).astype(jnp.bfloat16)
    chosen = jnp.dot(reorder, onehot, preferred_element_type=jnp.float32)
    chosen_bf = chosen.astype(jnp.bfloat16)
    partial_sums = jnp.dot(chosen_bf, flattened, preferred_element_type=jnp.float32)
    partial_counts = jnp.sum(chosen, axis=1)
    total_sums, total_counts = lax.psum((partial_sums, partial_counts), "tm")
    all_mean = (total_sums / total_counts[:, None]).astype(jnp.bfloat16)
    own_rows = bin_total // lax.axis_size("tm")
    own_mean = lax.dynamic_slice_in_dim(all_mean, lax.axis_index("tm") * own_rows, own_rows, 0)
    phase_mean = own_mean.reshape(own_mean.shape[0], 3, cell_count)
    row_numbers = jnp.arange(bin_total, dtype=jnp.int32)
    inverse = jnp.zeros((bin_total,), jnp.int32).at[owner_order].set(row_numbers)
    mean_by_bin = jnp.take(all_mean, inverse, axis=0)
    match_int = matches.astype(jnp.int32)
    ranks = jnp.cumsum(match_int, axis=1) - 1
    slot = jnp.sum(match_int * ranks, axis=0)
    target = phase_bin * capacity + slot
    snap_numbers = jnp.arange(snap_rows, dtype=jnp.int32)
    source = jnp.full((bin_total * capacity,), snap_rows, jnp.int32).at[target].set(snap_numbers)
    gathered = jnp.take(flattened, source, axis=0, mode="fill", fill_value=0)
    gathered = gathered.reshape(bin_total, capacity, width)
    grouped = (gathered.astype(jnp.float32) - mean_by_bin.astype(jnp.float32)[:, None, :]).astype(
        jnp.bfloat16
    )
    modes_flat = modes.reshape(bin_total, mode_count, width)
    products = lax.dot_general(
        grouped, modes_flat, (((2,), (2,)), ((0,), (0,))), preferred_element_type=jnp.float32
    )
    picked = jnp.take(products.reshape(bin_total * capacity, mode_count), target, axis=0)
    coefficients = lax.psum(picked, "space")
    return (phase_mean, coefficients)


def solution(mesh):
    in_specs = (P("tm", None, "space"), P("tm"), P(), P(None, None, None, "space"))
    out_specs = (P("tm", None, "space"), P("tm", None))
    return jax.shard_map(
        on_device, mesh=mesh, in_specs=in_specs, out_specs=out_specs, check_vma=False
    )
```

profile of v0, /device:TPU:0, one launch (start us, length us, event | category | flops | bytes accessed | tf_op | source)
XLA Modules:
  0.0 239.0 jit_solution(14934051923834580583)
XLA Ops:
  7.2 0.0 copy-start
  7.2 0.0 copy-start.1
  7.2 0.0 all-reduce.3.cloned.1.call-start
  7.2 16.7 %copy.9 = bf16[1024,3,2048]{0,2,1:T(8,128)(2,1)} copy(bf16[1024,3,2048]{2,0,1:T(8,128)(2,1)} %param.4) | data formatting | bytes 25165824 | tf_op args[0]
  23.9 0.0 copy-done
  23.9 0.0 copy-done.1
  23.9 0.3 fusion.17
  24.2 8.7 %fusion.7 = f32[16,6144]{1,0:T(8,128)} fusion(bf16[1024,6144]{0,1:T(8,128)(2,1)} %bitcast.19, bf16[16,1024]{1,0:T(8,128)(2,1)S(1)} %get-tuple-element.5), kind=kOutput, calls=%fused_computation.19 | convolution fusion | flops 201326592 | bytes 13008896 | tf_op jit(solution)/shard_map/dot_general | solution.py:21
  32.9 0.0 all-reduce.3.cloned.1.call-update
  32.9 0.0 all-reduce.5.cloned.1.call-start
  33.0 16.7 %copy.12 = bf16[1024,6144]{1,0:T(8,128)(2,1)} copy(bf16[1024,6144]{0,1:T(8,128)(2,1)} %bitcast.20) | data formatting | bytes 25165824 | tf_op jit(solution)/shard_map/reshape | solution.py:14
  49.7 0.6 scatter_custom_fusion.1
  50.3 13.5 %psum.22 = f32[16]{0:T(128)S(1)} all-reduce(f32[16]{0:T(128)S(1)} %get-tuple-element.4), channel_id=1, replica_groups=mesh['tm'=4,'space'=8] {'tm'}, use_global_device_ids=true, to_apply=%region_2.0 | all-reduce | flops 16 | bytes 128 | tf_op jit(solution)/shard_map/psum | solution.py:23
  63.8 4.5 %reduce-window.6 = s32[16,8,128]{2,1,0:T(8,128)S(1)} reduce-window(s32[16,8,128]{2,1,0:T(8,128)S(1)} %fusion.5, s32[]{:T(128)} %constant.40.clone.1), window={size=1x1x128 pad=0_0x0_0x127_0}, to_apply=%region_3.0 | reduce-window | flops 2080768 | bytes 131076 | tf_op jit(solution)/shard_map/reduce-window
  68.4 0.1 slice.14
  68.4 0.1 copy.10
  68.6 0.1 copy.11
  68.7 0.1 select_reduce_fusion
  68.8 4.5 %scatter_custom_fusion = s32[2048]{0:T(1024)S(1)} fusion(s32[1024]{0:T(1024)S(1)} %get-tuple-element.3, s32[1024]{0:T(1024)S(1)} %iota.22, s32[]{:T(128)} %constant.65.clone.1), kind=kCustom, calls=%fused_computation.29 | custom fusion | bytes 8196 | tf_op jit(solution)/shard_map/scatter | solution.py:36
  73.3 32.6 %copy.13 = bf16[16,128,3,2048]{1,3,2,0:T(8,128)(2,1)} copy(bf16[16,128,3,2048]{3,1,2,0:T(8,128)(2,1)} %param.7) | data formatting | bytes 50331648 | tf_op args[3]
  106.0 48.0 %gather_fusion = bf16[2048,6144]{1,0:T(8,128)(2,1)} fusion(bf16[1024,6144]{1,0:T(8,128)(2,1)} %copy.12, s32[2048]{0:T(1024)S(1)} %fusion.10), kind=kCustom, calls=%fused_computation | custom fusion | bytes 50339840 | tf_op jit(solution)/shard_map/jit(_take)/gather | solution.py:37
  154.0 0.0 all-reduce.3.cloned.1.call-done
  154.0 1.1 divide_convert_fusion
  155.1 0.7 gather_fusion.1
  155.8 0.1 select_convert_fusion
  155.9 17.7 %fusion = f32[16,128,128]{2,1,0:T(8,128)S(1)} fusion(bf16[16,128,6144]{1,2,0:T(8,128)(2,1)} %bitcast.21, f32[16,6144]{1,0:T(8,128)S(1)} %select_convert_fusion, bf16[16,128,6144]{2,1,0:T(8,128)(2,1)} %bitcast.22, pred[16,128]{1,0:T(8,128)(4,1)S(1)} %and_bitcast_fusion), kind=kOutput, calls=%fused_computation.6 | convolution fusion | flops 3271557120 | bytes 51775488 | tf_op jit(solution)/shard_map/dot_general | solution.py:43
  173.6 2.8 %gather_fusion.2 = f32[1024,128]{1,0:T(8,128)S(1)} fusion(f32[2048,128]{1,0:T(8,128)S(1)} %bitcast.23, s32[1024]{0:T(1024)S(1)} %broadcast_clamp_fusion), kind=kCustom, calls=%fused_computation.2 | custom fusion | bytes 1052672 | tf_op jit(solution)/shard_map/jit(_take)/gather | solution.py:46
  176.4 1.0 broadcast_select_fusion
  177.4 0.0 all-reduce.5.cloned.1.call-update
  177.4 0.7 constant_dynamic-slice_fusion
  178.1 52.2 %all-reduce.5.cloned.1.call-done = f32[1024,128]{1,0:T(8,128)} async-done(((f32[1024,128]{1,0:T(8,128)}), f32[1024,128]{1,0:T(8,128)}) %all-reduce.5.cloned.1.call-update) | async-done | bytes 524304 | tf_op jit(solution)/shard_map/psum | solution.py:47
  230.3 1.9 copy.18
  (13 shorter events, 0.1 us)
Async XLA Ops:
  7.2 16.8 %copy-start = (s32[1024]{0:T(1024)S(1)}, s32[1024]{0:T(1024)}, u32[]{:S(2)}) copy-start(s32[1024]{0:T(1024)} %param.5) | copy-start | bytes 12292
  7.2 16.7 %copy-start.1 = (s32[16]{0:T(128)S(1)}, s32[16]{0:T(128)}, u32[]{:S(2)}) copy-start(s32[16]{0:T(128)} %param.6) | copy-start | bytes 196
  7.2 146.8 %all-reduce.3.cloned.1.call-start = ((), (), s32[]{:S(2)}) async-start(), calls=%async_computation | async-start | bytes 786432 | tf_op jit(solution)/shard_map/psum | solution.py:23
  32.9 197.3 %all-reduce.5.cloned.1.call-start = ((), (), s32[]{:S(2)}) async-start(), calls=%async_computation.1 | async-start | bytes 1048576 | tf_op jit(solution)/shard_map/psum | solution.py:47
Sparse Core Ops, SparseCore 0:
  33.1 39.8 all-reduce.2
  177.5 52.6 all-reduce.4
where the time goes:
time: 241 us; the launch traced here: 239 us
  local copies, waits for them, and re-layouts  125 us (52%)
  waiting for transfers between devices  52.2 us (22%)
  matrix products  26.7 us (11%)
  between operations  14.2 us (6%)
  blocking collectives  13.5 us (6%)
  other arithmetic  6.89 us (3%)
    psum x1, waiting for transfers between devices, on_device(): coefficients = lax.psum(picked, 'space')  52.2 us
    unnamed x7, local copies, waits for them, and re-layouts  51.2 us
    gather x1, local copies, waits for them, and re-layouts, on_device(): gathered = jnp.take(flattened, source, axis=0, mode='fill', fill_value=0)  48 us
    dot_general x1, matrix products, on_device(): lax.dot_general(grouped, modes_flat, (((2,), (2,)), ((0,), (0,))), prefer...  17.7 us
    reshape x1, local copies, waits for them, and re-layouts, on_device(): flattened = snaps.reshape(snap_rows, width)  16.7 us
    psum x1, blocking collectives, on_device(): total_sums, total_counts = lax.psum((partial_sums, partial_counts), 'tm')  13.5 us
    dot_general x1, matrix products, on_device(): jnp.dot(chosen_bf, flattened, preferred_element_type=jnp.float32)  8.7 us
  transfers between devices with their start and end apart: 2, of which 1 were waited for; matrix products, arithmetic and copies ran while one was open for 45% of the time, Pallas kernels for 0%

commit v1 on v0

--- a/solution.py
+++ b/solution.py
@@ -44,7 +44,11 @@
         grouped, modes_flat, (((2,), (2,)), ((0,), (0,))), preferred_element_type=jnp.float32
     )
     picked = jnp.take(products.reshape(bin_total * capacity, mode_count), target, axis=0)
-    coefficients = lax.psum(picked, "space")
+    coefficients = picked
+    for hop in (1, 2, 4):
+        coefficients = coefficients + lax.ppermute(
+            coefficients, "space", [(dev, dev ^ hop) for dev in range(8)]
+        )
     return (phase_mean, coefficients)
 
 

time: 241 us -> 215 us (0.89)
  waiting for transfers between devices: 52.2 us -> 25.2 us
  starting transfers between devices: 0.08 us -> 3.44 us
    psum x1 -> x0, waiting for transfers between devices: 52.2 us -> none  [on_device(): coefficients = lax.psum(picked, 'space')]
    ppermute x0 -> x3, waiting for transfers between devices: none -> 25.1 us  [on_device(): lax.ppermute(coefficients, 'space', [(dev, dev ^ hop) for dev in range(8)])]
    ppermute x0 -> x3, starting transfers between devices: none -> 3.4 us  [on_device(): lax.ppermute(coefficients, 'space', [(dev, dev ^ hop) for dev in range(8)])]
    unnamed x7 -> x6, local copies, waits for them, and re-layouts: 51.2 us -> 49.3 us
  transfers between devices with their start and end apart: 2 -> 4, of which waited for: 1 -> 3; matrix products, arithmetic and copies ran while one was open for 45% -> 51% of each run, Pallas kernels for 0% -> 0%
where the time goes in v1:
time: 215 us; the launch traced here: 214 us
  local copies, waits for them, and re-layouts  124 us (58%)
  matrix products  26.7 us (12%)
  waiting for transfers between devices  25.2 us (12%)
  between operations  14.2 us (7%)
  blocking collectives  13.4 us (6%)
  other arithmetic  7.19 us (3%)
  starting transfers between devices  3.44 us (2%)
    unnamed x6, local copies, waits for them, and re-layouts  49.3 us
    gather x1, local copies, waits for them, and re-layouts, on_device(): gathered = jnp.take(flattened, source, axis=0, mode='fill', fill_value=0)  48 us
    ppermute x3, waiting for transfers between devices, on_device(): lax.ppermute(coefficients, 'space', [(dev, dev ^ hop) for dev in range(8)])  25.1 us
    dot_general x1, matrix products, on_device(): lax.dot_general(grouped, modes_flat, (((2,), (2,)), ((0,), (0,))), prefer...  17.7 us
    reshape x1, local copies, waits for them, and re-layouts, on_device(): flattened = snaps.reshape(snap_rows, width)  16.7 us
    psum x1, blocking collectives, on_device(): total_sums, total_counts = lax.psum((partial_sums, partial_counts), 'tm')  13.4 us
    dot_general x1, matrix products, on_device(): jnp.dot(chosen_bf, flattened, preferred_element_type=jnp.float32)  8.7 us
    another operation x2, other arithmetic  4.55 us
  transfers between devices with their start and end apart: 4, of which 3 were waited for; matrix products, arithmetic and copies ran while one was open for 51% of the time, Pallas kernels for 0%

profile of v1, /device:TPU:0, one launch (start us, length us, event | category | flops | bytes accessed | tf_op | source)
XLA Modules:
  0.0 213.6 jit_solution(15479498690608505950)
XLA Ops:
  7.2 0.0 copy-start
  7.2 0.0 copy-start.1
  7.2 0.0 all-reduce.2.cloned.1.call-start
  7.2 16.7 %copy.9 = bf16[1024,3,2048]{0,2,1:T(8,128)(2,1)} copy(bf16[1024,3,2048]{2,0,1:T(8,128)(2,1)} %param.4) | data formatting | bytes 25165824 | tf_op args[0]
  23.9 0.0 copy-done
  23.9 0.0 copy-done.1
  23.9 0.3 fusion.17
  24.2 8.7 %fusion.7 = f32[16,6144]{1,0:T(8,128)} fusion(bf16[1024,6144]{0,1:T(8,128)(2,1)} %bitcast.19, bf16[16,1024]{1,0:T(8,128)(2,1)S(1)} %get-tuple-element.5), kind=kOutput, calls=%fused_computation.19 | convolution fusion | flops 201326592 | bytes 13008896 | tf_op jit(solution)/shard_map/dot_general | solution.py:21
  32.9 0.0 all-reduce.2.cloned.1.call-update
  33.0 16.7 %copy.12 = bf16[1024,6144]{1,0:T(8,128)(2,1)} copy(bf16[1024,6144]{0,1:T(8,128)(2,1)} %bitcast.20) | data formatting | bytes 25165824 | tf_op jit(solution)/shard_map/reshape | solution.py:14
  49.6 0.6 scatter_custom_fusion.1
  50.3 13.4 %psum.15 = f32[16]{0:T(128)S(1)} all-reduce(f32[16]{0:T(128)S(1)} %get-tuple-element.4), channel_id=1, replica_groups=mesh['tm'=4,'space'=8] {'tm'}, use_global_device_ids=true, to_apply=%region_2.0 | all-reduce | flops 16 | bytes 128 | tf_op jit(solution)/shard_map/psum | solution.py:23
  63.7 4.5 %reduce-window.6 = s32[16,8,128]{2,1,0:T(8,128)S(1)} reduce-window(s32[16,8,128]{2,1,0:T(8,128)S(1)} %fusion.5, s32[]{:T(128)} %constant.40.clone.1), window={size=1x1x128 pad=0_0x0_0x127_0}, to_apply=%region_3.0 | reduce-window | flops 2080768 | bytes 131076 | tf_op jit(solution)/shard_map/reduce-window
  68.2 0.1 slice.14
  68.3 0.1 copy.10
  68.5 0.1 copy.11
  68.5 0.1 select_reduce_fusion
  68.7 4.5 %scatter_custom_fusion = s32[2048]{0:T(1024)S(1)} fusion(s32[1024]{0:T(1024)S(1)} %get-tuple-element.3, s32[1024]{0:T(1024)S(1)} %iota.22, s32[]{:T(128)} %constant.65.clone.1), kind=kCustom, calls=%fused_computation.29 | custom fusion | bytes 8196 | tf_op jit(solution)/shard_map/scatter | solution.py:36
  73.2 32.6 %copy.13 = bf16[16,128,3,2048]{1,3,2,0:T(8,128)(2,1)} copy(bf16[16,128,3,2048]{3,1,2,0:T(8,128)(2,1)} %param.7) | data formatting | bytes 50331648 | tf_op args[3]
  105.8 48.0 %gather_fusion = bf16[2048,6144]{1,0:T(8,128)(2,1)} fusion(bf16[1024,6144]{1,0:T(8,128)(2,1)} %copy.12, s32[2048]{0:T(1024)S(1)} %fusion.10), kind=kCustom, calls=%fused_computation | custom fusion | bytes 50339840 | tf_op jit(solution)/shard_map/jit(_take)/gather | solution.py:37
  153.8 0.0 all-reduce.2.cloned.1.call-done
  153.9 1.1 divide_convert_fusion
  154.9 0.7 gather_fusion.1
  155.6 0.1 select_convert_fusion
  155.7 17.7 %fusion = f32[16,128,128]{2,1,0:T(8,128)S(1)} fusion(bf16[16,128,6144]{1,2,0:T(8,128)(2,1)} %bitcast.21, f32[16,6144]{1,0:T(8,128)S(1)} %select_convert_fusion, bf16[16,128,6144]{2,1,0:T(8,128)(2,1)} %bitcast.22, pred[16,128]{1,0:T(8,128)(4,1)S(1)} %and_bitcast_fusion), kind=kOutput, calls=%fused_computation.6 | convolution fusion | flops 3271557120 | bytes 51775488 | tf_op jit(solution)/shard_map/dot_general | solution.py:43
  173.4 2.8 %gather_fusion.2 = f32[1024,128]{1,0:T(8,128)S(1)} fusion(f32[2048,128]{1,0:T(8,128)S(1)} %bitcast.23, s32[1024]{0:T(1024)S(1)} %broadcast_clamp_fusion), kind=kCustom, calls=%fused_computation.2 | custom fusion | bytes 1052672 | tf_op jit(solution)/shard_map/jit(_take)/gather | solution.py:46
  176.2 0.2 broadcast_select_fusion
  176.5 0.1 collective-permute-start
  176.5 1.9 collective-permute-done
  178.4 0.2 fusion.21
  178.6 1.7 collective-permute-start.1
  180.3 12.4 %collective-permute-done.1 = f32[1024,128]{1,0:T(8,128)S(1)} collective-permute-done((f32[1024,128]{1,0:T(8,128)S(1)}, f32[1024,128]{1,0:T(8,128)S(1)}, u32[]{:S(2)}, u32[]{:S(2)}) %collective-permute-start.1) | collective-permute-done | bytes 524320 | tf_op jit(solution)/shard_map/ppermute | solution.py:49
  192.7 0.1 add.52
  192.7 1.7 collective-permute-start.2
  194.4 0.6 constant_dynamic-slice_fusion
  195.1 10.9 %collective-permute-done.2 = f32[1024,128]{1,0:T(8,128)S(1)} collective-permute-done((f32[1024,128]{1,0:T(8,128)S(1)}, f32[1024,128]{1,0:T(8,128)S(1)}, u32[]{:S(2)}, u32[]{:S(2)}) %collective-permute-start.2) | collective-permute-done | bytes 524320 | tf_op jit(solution)/shard_map/ppermute | solution.py:49
  205.9 0.8 add.53
  (13 shorter events, 0.1 us)
Async XLA Ops:
  7.2 16.8 %copy-start = (s32[1024]{0:T(1024)S(1)}, s32[1024]{0:T(1024)}, u32[]{:S(2)}) copy-start(s32[1024]{0:T(1024)} %param.5) | copy-start | bytes 12292
  7.2 16.7 %copy-start.1 = (s32[16]{0:T(128)S(1)}, s32[16]{0:T(128)}, u32[]{:S(2)}) copy-start(s32[16]{0:T(128)} %param.6) | copy-start | bytes 196
  7.2 146.7 %all-reduce.2.cloned.1.call-start = ((), (), s32[]{:S(2)}) async-start(), calls=%async_computation | async-start | bytes 786432 | tf_op jit(solution)/shard_map/psum | solution.py:23
  176.5 2.0 collective-permute-start
  178.6 14.0 %collective-permute-start.1 = (f32[1024,128]{1,0:T(8,128)S(1)}, f32[1024,128]{1,0:T(8,128)S(1)}, u32[]{:S(2)}, u32[]{:S(2)}) collective-permute-start(f32[1024,128]{1,0:T(8,128)S(1)} %fusion.21), channel_id=1, source_target_pairs={{0,2},{1,3},{2,0},{3,1},{4,6},{5,7},{6,4},{7,5},{8,10},{9,11},{10,... | collective-permute-start | bytes 1572872 | tf_op jit(solution)/shard_map/ppermute | solution.py:49
  192.7 13.2 %collective-permute-start.2 = (f32[1024,128]{1,0:T(8,128)S(1)}, f32[1024,128]{1,0:T(8,128)S(1)}, u32[]{:S(2)}, u32[]{:S(2)}) collective-permute-start(f32[1024,128]{1,0:T(8,128)S(1)} %add.52), channel_id=1, source_target_pairs={{0,4},{1,5},{2,6},{3,7},{4,0},{5,1},{6,2},{7,3},{8,12},{9,13},{10,... | collective-permute-start | bytes 1572872 | tf_op jit(solution)/shard_map/ppermute | solution.py:49
Sparse Core Ops, SparseCore 0:
  33.1 39.7 all-reduce.1
